TPU v7x, 512 devices: a whole 4x8x8 slice. The times are simulated.
512 devices in a mesh: gx: 32 (over z, x_lo, core), gy: 16 (over y, x_hi).
Axes of the slice: x: 4 (x_hi: 2, x_lo: 2; x = x_hi * 2 + x_lo), y: 8, z: 8, core: 2. Of those that a mesh axis runs over, the one named last changes fastest.
Arguments:
- green: bfloat16 [32, 16, 1024, 1024], P('gx', 'gy'), may hold values from -0.1875 to 0.1875
- sources: bfloat16 [6, 32, 16, 768, 128], P(None, 'gx', 'gy'), may hold values from -3 to 3
- entering: float32 [32, 16, 1024, 128], P('gx', 'gy'), may hold values from -6 to 6
- start_front: int32 [24], replicated, may hold values from -5 to 41, as said below
Outputs:
- last_traces: float32 [32, 16, 1024, 128], P('gx', 'gy')
Inputs may be any that keep to these rules, and one draw needn't show every extreme that they name: `start_front`: the 24 values are distinct.
All inputs are finite; a program needn't handle non-finite values.
Results may differ from a plain program's by a relative error of at most 0.0055.
Values may be sent and summed in bfloat16 or wider, within the bound.
A program may use at most 64 MiB of HBM per device.

v0:
```python
import jax
import jax.numpy as jnp
from jax import lax
from jax.sharding import PartitionSpec as P


def passed_along(shard, axis, by):
    size = lax.axis_size(axis)
    pairs = [(i, i + by) for i in range(size) if 0 <= i + by < size]
    return lax.ppermute(shard, axis, pairs)


def local(green, sources, entering, start_front):
    operator = green[0, 0]
    tick_total = sources.shape[0]
    edge_rows = sources.shape[3]
    trace_rows = edge_rows // 2
    corner_rows = operator.shape[0] - edge_rows
    width = entering.shape[3]
    front_index = lax.axis_index("gx") + lax.axis_index("gy")
    rounded = entering[0, 0].astype(jnp.bfloat16)
    corner_zeros = jnp.zeros((corner_rows, width), jnp.float32)
    traces = entering[0, 0]
    for step_index in range(tick_total):
        if step_index > 0:
            outgoing = traces.astype(jnp.bfloat16)
            east_part = outgoing[:trace_rows]
            north_part = outgoing[trace_rows:edge_rows]
            corner_part = outgoing[edge_rows:]
            west_in = passed_along(east_part, "gx", 1)
            south_in = passed_along(north_part, "gy", 1)
            across = passed_along(corner_part, "gx", 1)
            diagonal = passed_along(across, "gy", 1)
            rounded = jnp.concatenate([west_in, south_in, diagonal], axis=0)
        product = jnp.dot(operator, rounded, preferred_element_type=jnp.float32)
        source_term = jnp.concatenate(
            [sources[step_index, 0, 0].astype(jnp.float32), corner_zeros], axis=0
        )
        is_live = jnp.any(start_front == front_index - step_index)
        traces = jnp.where(is_live, product + source_term, jnp.zeros_like(product))
    return traces[None, None]


def solution(mesh):
    in_specs = (
        P("gx", "gy", None, None),
        P(None, "gx", "gy", None, None),
        P("gx", "gy", None, None),
        P(),
    )
    out_specs = P("gx", "gy", None, None)
    return jax.shard_map(local, mesh=mesh, in_specs=in_specs, out_specs=out_specs, check_vma=False)
```

profile of v0, /device:TPU:144, one launch (start us, length us, event | category | flops | bytes accessed | tf_op | source)
XLA Modules:
  0.0 107.6 jit_solution(7632538338452668245)
XLA Ops:
  0.0 1.6 %slice_bitcast_fusion = (bf16[768,128]{1,0:T(8,128)(2,1)S(1)}, bf16[768,128]{1,0:T(8,128)(2,1)S(1)}, bf16[768,128]{1,0:T(8,128)(2,1)S(1)}, bf16[768,128]{1,0:T(8...) fusion(bf16[6,1,1,768,128]{4,3,2,1,0:T(8,128)(2,1)} %param.5), kind=kLoop, calls=%fused_computation.62 | loop fusion | bytes 2359296 | tf_op jit(solution)/shard_map/convert_element_type | solution.py:37
  1.6 0.8 compare_reduce_fusion.5
  2.4 1.3 %fusion.66 = bf16[1024,128]{1,0:T(8,128)(2,1)S(1)} fusion(bf16[1,1,1024,1024]{3,2,1,0:T(8,128)(2,1)S(1)} %copy-done, bf16[768,128]{1,0:T(8,128)(2,1)S(1)} %get-tuple-element.15, f32[1,1,1024,128]{3,2,1,0:T(8,128)S(1)} %copy-done.1, pred[]{:T(512)} %get-tuple-element.9), kind=kOutput, calls=%fused_computation.30 | convolution fusion | flops 269090816 | bytes 3080193 | tf_op jit(solution)/shard_map/dot_general | solution.py:35
  3.7 1.9 %collective-permute-start.2 = (bf16[256,128]{1,0:T(8,128)(2,1)S(1)}, bf16[256,128]{1,0:T(8,128)(2,1)S(1)}, u32[]{:S(2)}, u32[]{:S(2)}) collective-permute-start(bf16[256,128]{1,0:T(8,128)(2,1)S(1)} %slice.86), channel_id=1, source_target_pairs={{0,16},{16,32},{32,48},{48,64},{64,80},{80,96},{96,112},{112,128},... | collective-permute-start | bytes 196616 | tf_op jit(solution)/shard_map/ppermute | solution.py:10
  5.7 3.5 %collective-permute-start = (bf16[384,128]{1,0:T(8,128)(2,1)S(1)}, bf16[384,128]{1,0:T(8,128)(2,1)S(1)}, u32[]{:S(2)}, u32[]{:S(2)}) collective-permute-start(bf16[384,128]{1,0:T(8,128)(2,1)S(1)} %get-tuple-element.25), channel_id=1, source_target_pairs={{0,16},{16,32},{32,48},{48,64},{64,80},{80,96},{96,112},{112,128},... | collective-permute-start | bytes 294920 | tf_op jit(solution)/shard_map/ppermute | solution.py:10
  9.2 4.6 %collective-permute-start.1 = (bf16[384,128]{1,0:T(8,128)(2,1)S(1)}, bf16[384,128]{1,0:T(8,128)(2,1)S(1)}, u32[]{:S(2)}, u32[]{:S(2)}) collective-permute-start(bf16[384,128]{1,0:T(8,128)(2,1)S(1)} %get-tuple-element.26), channel_id=1, source_target_pairs={{0,1},{1,2},{2,3},{3,4},{4,5},{5,6},{6,7},{7,8},{8,9},{9,10},{10,1... | collective-permute-start | bytes 294920 | tf_op jit(solution)/shard_map/ppermute | solution.py:10
  13.8 0.0 collective-permute-done.2
  13.8 3.7 %collective-permute-start.3 = (bf16[256,128]{1,0:T(8,128)(2,1)S(1)}, bf16[256,128]{1,0:T(8,128)(2,1)S(1)}, u32[]{:S(2)}, u32[]{:S(2)}) collective-permute-start(bf16[256,128]{1,0:T(8,128)(2,1)S(1)} %collective-permute-done.2), channel_id=1, source_target_pairs={{0,1},{1,2},{2,3},{3,4},{4,5},{5,6},{6,7},{7,8},{8,9},{9,10},{10,1... | collective-permute-start | bytes 196616 | tf_op jit(solution)/shard_map/ppermute | solution.py:10
  17.6 0.0 collective-permute-done
  17.6 0.6 collective-permute-done.1
  18.2 4.2 %collective-permute-done.3 = bf16[256,128]{1,0:T(8,128)(2,1)S(1)} collective-permute-done((bf16[256,128]{1,0:T(8,128)(2,1)S(1)}, bf16[256,128]{1,0:T(8,128)(2,1)S(1)}, u32[]{:S(2)}, u32[]{:S(2)}) %collective-permute-start.3) | collective-permute-done | bytes 65568 | tf_op jit(solution)/shard_map/ppermute | solution.py:10
  22.4 1.3 %fusion.78 = bf16[1024,128]{1,0:T(8,128)(2,1)S(1)} fusion(bf16[1,1,1024,1024]{3,2,1,0:T(8,128)(2,1)S(1)} %copy-done, bf16[256,128]{1,0:T(8,128)(2,1)S(1)} %collective-permute-done.3, bf16[384,128]{1,0:T(8,128)(2,1)S(1)} %collective-permute-done.1, bf16[384,128]{1,0:T(8,128)(2,1)S(1)} %collective-permute-done, bf16[768,128]{1,0:T(8,128)(2,1)S(1)} %get-tuple-element.14, ...), kind=kOutput, calls=%fused_computation.34 | convolution fusion | flops 269746176 | bytes 2818049 | tf_op jit(solution)/shard_map/dot_general | solution.py:35
  23.8 1.9 %collective-permute-start.6 = (bf16[256,128]{1,0:T(8,128)(2,1)S(1)}, bf16[256,128]{1,0:T(8,128)(2,1)S(1)}, u32[]{:S(2)}, u32[]{:S(2)}) collective-permute-start(bf16[256,128]{1,0:T(8,128)(2,1)S(1)} %slice.89), channel_id=1, source_target_pairs={{0,16},{16,32},{32,48},{48,64},{64,80},{80,96},{96,112},{112,128},... | collective-permute-start | bytes 196616 | tf_op jit(solution)/shard_map/ppermute | solution.py:10
  25.7 4.0 %collective-permute-start.4 = (bf16[384,128]{1,0:T(8,128)(2,1)S(1)}, bf16[384,128]{1,0:T(8,128)(2,1)S(1)}, u32[]{:S(2)}, u32[]{:S(2)}) collective-permute-start(bf16[384,128]{1,0:T(8,128)(2,1)S(1)} %get-tuple-element.23), channel_id=1, source_target_pairs={{0,16},{16,32},{32,48},{48,64},{64,80},{80,96},{96,112},{112,128},... | collective-permute-start | bytes 294920 | tf_op jit(solution)/shard_map/ppermute | solution.py:10
  29.8 3.7 %collective-permute-start.5 = (bf16[384,128]{1,0:T(8,128)(2,1)S(1)}, bf16[384,128]{1,0:T(8,128)(2,1)S(1)}, u32[]{:S(2)}, u32[]{:S(2)}) collective-permute-start(bf16[384,128]{1,0:T(8,128)(2,1)S(1)} %get-tuple-element.24), channel_id=1, source_target_pairs={{0,1},{1,2},{2,3},{3,4},{4,5},{5,6},{6,7},{7,8},{8,9},{9,10},{10,1... | collective-permute-start | bytes 294920 | tf_op jit(solution)/shard_map/ppermute | solution.py:10
  33.5 0.0 collective-permute-done.6
  33.5 4.6 %collective-permute-start.7 = (bf16[256,128]{1,0:T(8,128)(2,1)S(1)}, bf16[256,128]{1,0:T(8,128)(2,1)S(1)}, u32[]{:S(2)}, u32[]{:S(2)}) collective-permute-start(bf16[256,128]{1,0:T(8,128)(2,1)S(1)} %collective-permute-done.6), channel_id=1, source_target_pairs={{0,1},{1,2},{2,3},{3,4},{4,5},{5,6},{6,7},{7,8},{8,9},{9,10},{10,1... | collective-permute-start | bytes 196616 | tf_op jit(solution)/shard_map/ppermute | solution.py:10
  38.2 0.0 collective-permute-done.4
  38.2 0.6 collective-permute-done.5
  38.8 3.3 %collective-permute-done.7 = bf16[256,128]{1,0:T(8,128)(2,1)S(1)} collective-permute-done((bf16[256,128]{1,0:T(8,128)(2,1)S(1)}, bf16[256,128]{1,0:T(8,128)(2,1)S(1)}, u32[]{:S(2)}, u32[]{:S(2)}) %collective-permute-start.7) | collective-permute-done | bytes 65568 | tf_op jit(solution)/shard_map/ppermute | solution.py:10
  42.1 1.4 %fusion.75 = bf16[1024,128]{1,0:T(8,128)(2,1)S(1)} fusion(bf16[1,1,1024,1024]{3,2,1,0:T(8,128)(2,1)S(1)} %copy-done, bf16[256,128]{1,0:T(8,128)(2,1)S(1)} %collective-permute-done.7, bf16[384,128]{1,0:T(8,128)(2,1)S(1)} %collective-permute-done.5, bf16[384,128]{1,0:T(8,128)(2,1)S(1)} %collective-permute-done.4, bf16[768,128]{1,0:T(8,128)(2,1)S(1)} %get-tuple-element.13, ...), kind=kOutput, calls=%fused_computation.33 | convolution fusion | flops 269746176 | bytes 2818049 | tf_op jit(solution)/shard_map/dot_general | solution.py:35
  43.5 1.9 %collective-permute-start.10 = (bf16[256,128]{1,0:T(8,128)(2,1)S(1)}, bf16[256,128]{1,0:T(8,128)(2,1)S(1)}, u32[]{:S(2)}, u32[]{:S(2)}) collective-permute-start(bf16[256,128]{1,0:T(8,128)(2,1)S(1)} %slice.92), channel_id=1, source_target_pairs={{0,16},{16,32},{32,48},{48,64},{64,80},{80,96},{96,112},{112,128},... | collective-permute-start | bytes 196616 | tf_op jit(solution)/shard_map/ppermute | solution.py:10
  45.4 2.3 %collective-permute-start.8 = (bf16[384,128]{1,0:T(8,128)(2,1)S(1)}, bf16[384,128]{1,0:T(8,128)(2,1)S(1)}, u32[]{:S(2)}, u32[]{:S(2)}) collective-permute-start(bf16[384,128]{1,0:T(8,128)(2,1)S(1)} %get-tuple-element.21), channel_id=1, source_target_pairs={{0,16},{16,32},{32,48},{48,64},{64,80},{80,96},{96,112},{112,128},... | collective-permute-start | bytes 294920 | tf_op jit(solution)/shard_map/ppermute | solution.py:10
  47.7 5.8 %collective-permute-start.9 = (bf16[384,128]{1,0:T(8,128)(2,1)S(1)}, bf16[384,128]{1,0:T(8,128)(2,1)S(1)}, u32[]{:S(2)}, u32[]{:S(2)}) collective-permute-start(bf16[384,128]{1,0:T(8,128)(2,1)S(1)} %get-tuple-element.22), channel_id=1, source_target_pairs={{0,1},{1,2},{2,3},{3,4},{4,5},{5,6},{6,7},{7,8},{8,9},{9,10},{10,1... | collective-permute-start | bytes 294920 | tf_op jit(solution)/shard_map/ppermute | solution.py:10
  53.6 0.0 collective-permute-done.10
  53.6 4.4 %collective-permute-start.11 = (bf16[256,128]{1,0:T(8,128)(2,1)S(1)}, bf16[256,128]{1,0:T(8,128)(2,1)S(1)}, u32[]{:S(2)}, u32[]{:S(2)}) collective-permute-start(bf16[256,128]{1,0:T(8,128)(2,1)S(1)} %collective-permute-done.10), channel_id=1, source_target_pairs={{0,1},{1,2},{2,3},{3,4},{4,5},{5,6},{6,7},{7,8},{8,9},{9,10},{10,1... | collective-permute-start | bytes 196616 | tf_op jit(solution)/shard_map/ppermute | solution.py:10
  58.0 0.0 collective-permute-done.8
  58.0 0.0 collective-permute-done.9
  58.0 4.1 %collective-permute-done.11 = bf16[256,128]{1,0:T(8,128)(2,1)S(1)} collective-permute-done((bf16[256,128]{1,0:T(8,128)(2,1)S(1)}, bf16[256,128]{1,0:T(8,128)(2,1)S(1)}, u32[]{:S(2)}, u32[]{:S(2)}) %collective-permute-start.11) | collective-permute-done | bytes 65568 | tf_op jit(solution)/shard_map/ppermute | solution.py:10
  62.1 1.3 %fusion.72 = bf16[1024,128]{1,0:T(8,128)(2,1)S(1)} fusion(bf16[1,1,1024,1024]{3,2,1,0:T(8,128)(2,1)S(1)} %copy-done, bf16[256,128]{1,0:T(8,128)(2,1)S(1)} %collective-permute-done.11, bf16[384,128]{1,0:T(8,128)(2,1)S(1)} %collective-permute-done.9, bf16[384,128]{1,0:T(8,128)(2,1)S(1)} %collective-permute-done.8, ...), kind=kOutput, calls=%fused_computation.32 | convolution fusion | flops 269746176 | bytes 2818049 | tf_op jit(solution)/shard_map/dot_general | solution.py:35
  63.4 1.9 %collective-permute-start.14 = (bf16[256,128]{1,0:T(8,128)(2,1)S(1)}, bf16[256,128]{1,0:T(8,128)(2,1)S(1)}, u32[]{:S(2)}, u32[]{:S(2)}) collective-permute-start(bf16[256,128]{1,0:T(8,128)(2,1)S(1)} %slice.95), channel_id=1, source_target_pairs={{0,16},{16,32},{32,48},{48,64},{64,80},{80,96},{96,112},{112,128},... | collective-permute-start | bytes 196616 | tf_op jit(solution)/shard_map/ppermute | solution.py:10
  65.4 4.0 %collective-permute-start.12 = (bf16[384,128]{1,0:T(8,128)(2,1)S(1)}, bf16[384,128]{1,0:T(8,128)(2,1)S(1)}, u32[]{:S(2)}, u32[]{:S(2)}) collective-permute-start(bf16[384,128]{1,0:T(8,128)(2,1)S(1)} %get-tuple-element.19), channel_id=1, source_target_pairs={{0,16},{16,32},{32,48},{48,64},{64,80},{80,96},{96,112},{112,128},... | collective-permute-start | bytes 294920 | tf_op jit(solution)/shard_map/ppermute | solution.py:10
  69.4 6.2 %collective-permute-start.13 = (bf16[384,128]{1,0:T(8,128)(2,1)S(1)}, bf16[384,128]{1,0:T(8,128)(2,1)S(1)}, u32[]{:S(2)}, u32[]{:S(2)}) collective-permute-start(bf16[384,128]{1,0:T(8,128)(2,1)S(1)} %get-tuple-element.20), channel_id=1, source_target_pairs={{0,1},{1,2},{2,3},{3,4},{4,5},{5,6},{6,7},{7,8},{8,9},{9,10},{10,1... | collective-permute-start | bytes 294920 | tf_op jit(solution)/shard_map/ppermute | solution.py:10
  75.6 0.0 collective-permute-done.14
  75.6 4.6 %collective-permute-start.15 = (bf16[256,128]{1,0:T(8,128)(2,1)S(1)}, bf16[256,128]{1,0:T(8,128)(2,1)S(1)}, u32[]{:S(2)}, u32[]{:S(2)}) collective-permute-start(bf16[256,128]{1,0:T(8,128)(2,1)S(1)} %collective-permute-done.14), channel_id=1, source_target_pairs={{0,1},{1,2},{2,3},{3,4},{4,5},{5,6},{6,7},{7,8},{8,9},{9,10},{10,1... | collective-permute-start | bytes 196616 | tf_op jit(solution)/shard_map/ppermute | solution.py:10
  80.2 0.0 collective-permute-done.12
  80.3 0.0 collective-permute-done.13
  80.3 3.9 %collective-permute-done.15 = bf16[256,128]{1,0:T(8,128)(2,1)S(1)} collective-permute-done((bf16[256,128]{1,0:T(8,128)(2,1)S(1)}, bf16[256,128]{1,0:T(8,128)(2,1)S(1)}, u32[]{:S(2)}, u32[]{:S(2)}) %collective-permute-start.15) | collective-permute-done | bytes 65568 | tf_op jit(solution)/shard_map/ppermute | solution.py:10
  84.2 1.3 %fusion.69 = bf16[1024,128]{1,0:T(8,128)(2,1)S(1)} fusion(bf16[1,1,1024,1024]{3,2,1,0:T(8,128)(2,1)S(1)} %copy-done, bf16[256,128]{1,0:T(8,128)(2,1)S(1)} %collective-permute-done.15, bf16[384,128]{1,0:T(8,128)(2,1)S(1)} %collective-permute-done.13, bf16[384,128]{1,0:T(8,128)(2,1)S(1)} %collective-permute-done.12, ...), kind=kOutput, calls=%fused_computation.31 | convolution fusion | flops 269746176 | bytes 2818049 | tf_op jit(solution)/shard_map/dot_general | solution.py:35
  85.5 1.9 %collective-permute-start.18 = (bf16[256,128]{1,0:T(8,128)(2,1)S(1)}, bf16[256,128]{1,0:T(8,128)(2,1)S(1)}, u32[]{:S(2)}, u32[]{:S(2)}) collective-permute-start(bf16[256,128]{1,0:T(8,128)(2,1)S(1)} %slice.98), channel_id=1, source_target_pairs={{0,16},{16,32},{32,48},{48,64},{64,80},{80,96},{96,112},{112,128},... | collective-permute-start | bytes 196616 | tf_op jit(solution)/shard_map/ppermute | solution.py:10
  87.5 3.0 %collective-permute-start.16 = (bf16[384,128]{1,0:T(8,128)(2,1)S(1)}, bf16[384,128]{1,0:T(8,128)(2,1)S(1)}, u32[]{:S(2)}, u32[]{:S(2)}) collective-permute-start(bf16[384,128]{1,0:T(8,128)(2,1)S(1)} %get-tuple-element.17), channel_id=1, source_target_pairs={{0,16},{16,32},{32,48},{48,64},{64,80},{80,96},{96,112},{112,128},... | collective-permute-start | bytes 294920 | tf_op jit(solution)/shard_map/ppermute | solution.py:10
  90.5 6.4 %collective-permute-start.17 = (bf16[384,128]{1,0:T(8,128)(2,1)S(1)}, bf16[384,128]{1,0:T(8,128)(2,1)S(1)}, u32[]{:S(2)}, u32[]{:S(2)}) collective-permute-start(bf16[384,128]{1,0:T(8,128)(2,1)S(1)} %get-tuple-element.18), channel_id=1, source_target_pairs={{0,1},{1,2},{2,3},{3,4},{4,5},{5,6},{6,7},{7,8},{8,9},{9,10},{10,1... | collective-permute-start | bytes 294920 | tf_op jit(solution)/shard_map/ppermute | solution.py:10
  96.9 0.0 collective-permute-done.18
  96.9 2.2 %collective-permute-start.19 = (bf16[256,128]{1,0:T(8,128)(2,1)S(1)}, bf16[256,128]{1,0:T(8,128)(2,1)S(1)}, u32[]{:S(2)}, u32[]{:S(2)}) collective-permute-start(bf16[256,128]{1,0:T(8,128)(2,1)S(1)} %collective-permute-done.18), channel_id=1, source_target_pairs={{0,1},{1,2},{2,3},{3,4},{4,5},{5,6},{6,7},{7,8},{8,9},{9,10},{10,1... | collective-permute-start | bytes 196616 | tf_op jit(solution)/shard_map/ppermute | solution.py:10
  99.1 0.0 collective-permute-done.16
  99.1 0.4 collective-permute-done.17
  99.5 5.9 %collective-permute-done.19 = bf16[256,128]{1,0:T(8,128)(2,1)S(1)} collective-permute-done((bf16[256,128]{1,0:T(8,128)(2,1)S(1)}, bf16[256,128]{1,0:T(8,128)(2,1)S(1)}, u32[]{:S(2)}, u32[]{:S(2)}) %collective-permute-start.19) | collective-permute-done | bytes 65568 | tf_op jit(solution)/shard_map/ppermute | solution.py:10
  105.4 2.1 %fusion.57 = f32[1,1,1024,128]{3,2,1,0:T(8,128)} fusion(bf16[1,1,1024,1024]{3,2,1,0:T(8,128)(2,1)S(1)} %copy-done, bf16[256,128]{1,0:T(8,128)(2,1)S(1)} %collective-permute-done.19, bf16[384,128]{1,0:T(8,128)(2,1)S(1)} %collective-permute-done.17, bf16[384,128]{1,0:T(8,128)(2,1)S(1)} %collective-permute-done.16, ...), kind=kOutput, calls=%fused_computation.27 | convolution fusion | flops 269615104 | bytes 3080193 | tf_op jit(solution)/shard_map/dot_general | solution.py:35
  (16 shorter events, 0.1 us)
Async XLA Ops:
  0.0 2.4 %copy-start = (bf16[1,1,1024,1024]{3,2,1,0:T(8,128)(2,1)S(1)}, bf16[1,1,1024,1024]{3,2,1,0:T(8,128)(2,1)}, u32[]{:S(2)}) copy-start(bf16[1,1,1024,1024]{3,2,1,0:T(8,128)(2,1)} %param.4) | copy-start | bytes 6291460
  0.0 1.6 %copy-start.2 = (s32[24]{0:T(128)S(1)}, s32[24]{0:T(128)}, u32[]{:S(2)}) copy-start(s32[24]{0:T(128)} %param.7) | copy-start | bytes 292
  0.0 2.4 %copy-start.1 = (f32[1,1,1024,128]{3,2,1,0:T(8,128)S(1)}, f32[1,1,1024,128]{3,2,1,0:T(8,128)}, u32[]{:S(2)}) copy-start(f32[1,1,1024,128]{3,2,1,0:T(8,128)} %param.6) | copy-start | bytes 1572868
  3.7 10.1 %collective-permute-start.2 = (bf16[256,128]{1,0:T(8,128)(2,1)S(1)}, bf16[256,128]{1,0:T(8,128)(2,1)S(1)}, u32[]{:S(2)}, u32[]{:S(2)}) collective-permute-start(bf16[256,128]{1,0:T(8,128)(2,1)S(1)} %slice.86), channel_id=1, source_target_pairs={{0,16},{16,32},{32,48},{48,64},{64,80},{80,96},{96,112},{112,128},... | collective-permute-start | bytes 196616 | tf_op jit(solution)/shard_map/ppermute | solution.py:10
  5.7 11.9 %collective-permute-start = (bf16[384,128]{1,0:T(8,128)(2,1)S(1)}, bf16[384,128]{1,0:T(8,128)(2,1)S(1)}, u32[]{:S(2)}, u32[]{:S(2)}) collective-permute-start(bf16[384,128]{1,0:T(8,128)(2,1)S(1)} %get-tuple-element.25), channel_id=1, source_target_pairs={{0,16},{16,32},{32,48},{48,64},{64,80},{80,96},{96,112},{112,128},... | collective-permute-start | bytes 294920 | tf_op jit(solution)/shard_map/ppermute | solution.py:10
  9.2 9.0 %collective-permute-start.1 = (bf16[384,128]{1,0:T(8,128)(2,1)S(1)}, bf16[384,128]{1,0:T(8,128)(2,1)S(1)}, u32[]{:S(2)}, u32[]{:S(2)}) collective-permute-start(bf16[384,128]{1,0:T(8,128)(2,1)S(1)} %get-tuple-element.26), channel_id=1, source_target_pairs={{0,1},{1,2},{2,3},{3,4},{4,5},{5,6},{6,7},{7,8},{8,9},{9,10},{10,1... | collective-permute-start | bytes 294920 | tf_op jit(solution)/shard_map/ppermute | solution.py:10
  13.8 8.6 %collective-permute-start.3 = (bf16[256,128]{1,0:T(8,128)(2,1)S(1)}, bf16[256,128]{1,0:T(8,128)(2,1)S(1)}, u32[]{:S(2)}, u32[]{:S(2)}) collective-permute-start(bf16[256,128]{1,0:T(8,128)(2,1)S(1)} %collective-permute-done.2), channel_id=1, source_target_pairs={{0,1},{1,2},{2,3},{3,4},{4,5},{5,6},{6,7},{7,8},{8,9},{9,10},{10,1... | collective-permute-start | bytes 196616 | tf_op jit(solution)/shard_map/ppermute | solution.py:10
  23.8 9.8 %collective-permute-start.6 = (bf16[256,128]{1,0:T(8,128)(2,1)S(1)}, bf16[256,128]{1,0:T(8,128)(2,1)S(1)}, u32[]{:S(2)}, u32[]{:S(2)}) collective-permute-start(bf16[256,128]{1,0:T(8,128)(2,1)S(1)} %slice.89), channel_id=1, source_target_pairs={{0,16},{16,32},{32,48},{48,64},{64,80},{80,96},{96,112},{112,128},... | collective-permute-start | bytes 196616 | tf_op jit(solution)/shard_map/ppermute | solution.py:10
  25.7 12.4 %collective-permute-start.4 = (bf16[384,128]{1,0:T(8,128)(2,1)S(1)}, bf16[384,128]{1,0:T(8,128)(2,1)S(1)}, u32[]{:S(2)}, u32[]{:S(2)}) collective-permute-start(bf16[384,128]{1,0:T(8,128)(2,1)S(1)} %get-tuple-element.23), channel_id=1, source_target_pairs={{0,16},{16,32},{32,48},{48,64},{64,80},{80,96},{96,112},{112,128},... | collective-permute-start | bytes 294920 | tf_op jit(solution)/shard_map/ppermute | solution.py:10
  29.8 9.0 %collective-permute-start.5 = (bf16[384,128]{1,0:T(8,128)(2,1)S(1)}, bf16[384,128]{1,0:T(8,128)(2,1)S(1)}, u32[]{:S(2)}, u32[]{:S(2)}) collective-permute-start(bf16[384,128]{1,0:T(8,128)(2,1)S(1)} %get-tuple-element.24), channel_id=1, source_target_pairs={{0,1},{1,2},{2,3},{3,4},{4,5},{5,6},{6,7},{7,8},{8,9},{9,10},{10,1... | collective-permute-start | bytes 294920 | tf_op jit(solution)/shard_map/ppermute | solution.py:10
  33.5 8.6 %collective-permute-start.7 = (bf16[256,128]{1,0:T(8,128)(2,1)S(1)}, bf16[256,128]{1,0:T(8,128)(2,1)S(1)}, u32[]{:S(2)}, u32[]{:S(2)}) collective-permute-start(bf16[256,128]{1,0:T(8,128)(2,1)S(1)} %collective-permute-done.6), channel_id=1, source_target_pairs={{0,1},{1,2},{2,3},{3,4},{4,5},{5,6},{6,7},{7,8},{8,9},{9,10},{10,1... | collective-permute-start | bytes 196616 | tf_op jit(solution)/shard_map/ppermute | solution.py:10
  43.5 10.1 %collective-permute-start.10 = (bf16[256,128]{1,0:T(8,128)(2,1)S(1)}, bf16[256,128]{1,0:T(8,128)(2,1)S(1)}, u32[]{:S(2)}, u32[]{:S(2)}) collective-permute-start(bf16[256,128]{1,0:T(8,128)(2,1)S(1)} %slice.92), channel_id=1, source_target_pairs={{0,16},{16,32},{32,48},{48,64},{64,80},{80,96},{96,112},{112,128},... | collective-permute-start | bytes 196616 | tf_op jit(solution)/shard_map/ppermute | solution.py:10
  45.4 12.6 %collective-permute-start.8 = (bf16[384,128]{1,0:T(8,128)(2,1)S(1)}, bf16[384,128]{1,0:T(8,128)(2,1)S(1)}, u32[]{:S(2)}, u32[]{:S(2)}) collective-permute-start(bf16[384,128]{1,0:T(8,128)(2,1)S(1)} %get-tuple-element.21), channel_id=1, source_target_pairs={{0,16},{16,32},{32,48},{48,64},{64,80},{80,96},{96,112},{112,128},... | collective-permute-start | bytes 294920 | tf_op jit(solution)/shard_map/ppermute | solution.py:10
  47.7 10.3 %collective-permute-start.9 = (bf16[384,128]{1,0:T(8,128)(2,1)S(1)}, bf16[384,128]{1,0:T(8,128)(2,1)S(1)}, u32[]{:S(2)}, u32[]{:S(2)}) collective-permute-start(bf16[384,128]{1,0:T(8,128)(2,1)S(1)} %get-tuple-element.22), channel_id=1, source_target_pairs={{0,1},{1,2},{2,3},{3,4},{4,5},{5,6},{6,7},{7,8},{8,9},{9,10},{10,1... | collective-permute-start | bytes 294920 | tf_op jit(solution)/shard_map/ppermute | solution.py:10
  53.6 8.6 %collective-permute-start.11 = (bf16[256,128]{1,0:T(8,128)(2,1)S(1)}, bf16[256,128]{1,0:T(8,128)(2,1)S(1)}, u32[]{:S(2)}, u32[]{:S(2)}) collective-permute-start(bf16[256,128]{1,0:T(8,128)(2,1)S(1)} %collective-permute-done.10), channel_id=1, source_target_pairs={{0,1},{1,2},{2,3},{3,4},{4,5},{5,6},{6,7},{7,8},{8,9},{9,10},{10,1... | collective-permute-start | bytes 196616 | tf_op jit(solution)/shard_map/ppermute | solution.py:10
  63.4 12.2 %collective-permute-start.14 = (bf16[256,128]{1,0:T(8,128)(2,1)S(1)}, bf16[256,128]{1,0:T(8,128)(2,1)S(1)}, u32[]{:S(2)}, u32[]{:S(2)}) collective-permute-start(bf16[256,128]{1,0:T(8,128)(2,1)S(1)} %slice.95), channel_id=1, source_target_pairs={{0,16},{16,32},{32,48},{48,64},{64,80},{80,96},{96,112},{112,128},... | collective-permute-start | bytes 196616 | tf_op jit(solution)/shard_map/ppermute | solution.py:10
  65.4 14.9 %collective-permute-start.12 = (bf16[384,128]{1,0:T(8,128)(2,1)S(1)}, bf16[384,128]{1,0:T(8,128)(2,1)S(1)}, u32[]{:S(2)}, u32[]{:S(2)}) collective-permute-start(bf16[384,128]{1,0:T(8,128)(2,1)S(1)} %get-tuple-element.19), channel_id=1, source_target_pairs={{0,16},{16,32},{32,48},{48,64},{64,80},{80,96},{96,112},{112,128},... | collective-permute-start | bytes 294920 | tf_op jit(solution)/shard_map/ppermute | solution.py:10
  69.4 10.8 %collective-permute-start.13 = (bf16[384,128]{1,0:T(8,128)(2,1)S(1)}, bf16[384,128]{1,0:T(8,128)(2,1)S(1)}, u32[]{:S(2)}, u32[]{:S(2)}) collective-permute-start(bf16[384,128]{1,0:T(8,128)(2,1)S(1)} %get-tuple-element.20), channel_id=1, source_target_pairs={{0,1},{1,2},{2,3},{3,4},{4,5},{5,6},{6,7},{7,8},{8,9},{9,10},{10,1... | collective-permute-start | bytes 294920 | tf_op jit(solution)/shard_map/ppermute | solution.py:10
  75.6 8.6 %collective-permute-start.15 = (bf16[256,128]{1,0:T(8,128)(2,1)S(1)}, bf16[256,128]{1,0:T(8,128)(2,1)S(1)}, u32[]{:S(2)}, u32[]{:S(2)}) collective-permute-start(bf16[256,128]{1,0:T(8,128)(2,1)S(1)} %collective-permute-done.14), channel_id=1, source_target_pairs={{0,1},{1,2},{2,3},{3,4},{4,5},{5,6},{6,7},{7,8},{8,9},{9,10},{10,1... | collective-permute-start | bytes 196616 | tf_op jit(solution)/shard_map/ppermute | solution.py:10
  85.5 11.3 %collective-permute-start.18 = (bf16[256,128]{1,0:T(8,128)(2,1)S(1)}, bf16[256,128]{1,0:T(8,128)(2,1)S(1)}, u32[]{:S(2)}, u32[]{:S(2)}) collective-permute-start(bf16[256,128]{1,0:T(8,128)(2,1)S(1)} %slice.98), channel_id=1, source_target_pairs={{0,16},{16,32},{32,48},{48,64},{64,80},{80,96},{96,112},{112,128},... | collective-permute-start | bytes 196616 | tf_op jit(solution)/shard_map/ppermute | solution.py:10
  87.5 11.6 %collective-permute-start.16 = (bf16[384,128]{1,0:T(8,128)(2,1)S(1)}, bf16[384,128]{1,0:T(8,128)(2,1)S(1)}, u32[]{:S(2)}, u32[]{:S(2)}) collective-permute-start(bf16[384,128]{1,0:T(8,128)(2,1)S(1)} %get-tuple-element.17), channel_id=1, source_target_pairs={{0,16},{16,32},{32,48},{48,64},{64,80},{80,96},{96,112},{112,128},... | collective-permute-start | bytes 294920 | tf_op jit(solution)/shard_map/ppermute | solution.py:10
  90.5 9.0 %collective-permute-start.17 = (bf16[384,128]{1,0:T(8,128)(2,1)S(1)}, bf16[384,128]{1,0:T(8,128)(2,1)S(1)}, u32[]{:S(2)}, u32[]{:S(2)}) collective-permute-start(bf16[384,128]{1,0:T(8,128)(2,1)S(1)} %get-tuple-element.18), channel_id=1, source_target_pairs={{0,1},{1,2},{2,3},{3,4},{4,5},{5,6},{6,7},{7,8},{8,9},{9,10},{10,1... | collective-permute-start | bytes 294920 | tf_op jit(solution)/shard_map/ppermute | solution.py:10
  96.9 8.6 %collective-permute-start.19 = (bf16[256,128]{1,0:T(8,128)(2,1)S(1)}, bf16[256,128]{1,0:T(8,128)(2,1)S(1)}, u32[]{:S(2)}, u32[]{:S(2)}) collective-permute-start(bf16[256,128]{1,0:T(8,128)(2,1)S(1)} %collective-permute-done.18), channel_id=1, source_target_pairs={{0,1},{1,2},{2,3},{3,4},{4,5},{5,6},{6,7},{7,8},{8,9},{9,10},{10,1... | collective-permute-start | bytes 196616 | tf_op jit(solution)/shard_map/ppermute | solution.py:10
where the time goes:
time: 108 us
  starting transfers between devices  72.8 us (67%)
  waiting for transfers between devices  23.1 us (21%)
  matrix products  8.78 us (8%)
  local copies, waits for them, and re-layouts  1.68 us (2%)
    ppermute x20, starting transfers between devices, passed_along(): return lax.ppermute(shard, axis, pairs)  72.8 us
    ppermute x20, waiting for transfers between devices, passed_along(): return lax.ppermute(shard, axis, pairs)  23.1 us
    dot_general x6, matrix products, local(): product = jnp.dot(operator, rounded, preferred_element_type=jnp.float32)  8.78 us
  transfers between devices with their start and end apart: 20, of which 8 were waited for; matrix products, arithmetic and copies ran while one was open for 0% of the time, Pallas kernels for 0%

commit v1 on v0

v1 whole, which is shorter than its diff:
```python
import jax
import jax.numpy as jnp
from jax import lax
from jax.experimental import pallas as pl
from jax.experimental.pallas import tpu as pltpu
from jax.sharding import PartitionSpec as P

MESH = pl.DeviceIdType.MESH
LANES = 128
HALVES = 2
TILE = 256


def sweep_kernel(
    ticks, order, trace, width,
    fronts, green, sources, entering, last,
    operator, turned, source_rows, source_cols, first_in, sent, landed, held_half, result,
    green_sem, source_sem, entering_sem, last_sem, send_sem, land_sem,
):
    gx, gy = lax.axis_index("gx"), lax.axis_index("gy")
    columns, rows = lax.axis_size("gx"), lax.axis_size("gy")
    edge = 2 * trace
    half = width // HALVES
    blocks = order // LANES
    parts = (
        ("north", trace // LANES, edge // LANES, 0, 1),
        ("corner", edge // LANES, blocks, 1, 1),
        ("east", 0, trace // LANES, 1, 0),
    )
    tiles = [start for start in range(0, order, TILE)]
    tiles = [s for s in tiles if s + TILE > trace] + [s for s in tiles if s + TILE <= trace]

    def goes(dx, dy):
        ok = jnp.bool_(True)
        if dx:
            ok = jnp.logical_and(ok, gx < columns - 1)
        if dy:
            ok = jnp.logical_and(ok, gy < rows - 1)
        return ok

    def comes(dx, dy):
        ok = jnp.bool_(True)
        if dx:
            ok = jnp.logical_and(ok, gx > 0)
        if dy:
            ok = jnp.logical_and(ok, gy > 0)
        return ok

    barrier = pltpu.get_barrier_semaphore()
    for _, _, _, dx, dy in parts:
        @pl.when(comes(dx, dy))
        def _(dx=dx, dy=dy):
            pl.semaphore_signal(barrier, inc=1, device_id=(gx - dx, gy - dy), device_id_type=MESH)

    enter_copy = pltpu.make_async_copy(entering.at[0, 0], first_in, entering_sem)
    enter_copy.start()
    green_copies = {}
    for index, start in enumerate(tiles):
        copy = pltpu.make_async_copy(
            green.at[0, 0, pl.ds(start, TILE)], operator.at[pl.ds(start, TILE)], green_sem.at[index]
        )
        copy.start()
        green_copies[start] = copy
    source_copies = []
    for tick in range(ticks):
        copy = pltpu.make_async_copy(sources.at[tick, 0, 0], source_rows.at[tick], source_sem.at[tick])
        copy.start()
        source_copies.append(copy)

    for _, low, high, dx, dy in parts:
        @pl.when(jnp.logical_not(comes(dx, dy)))
        def _(low=low, high=high):
            landed[:, :, pl.ds(low, high - low)] = jnp.zeros(
                (ticks - 1, HALVES, high - low, half, LANES), jnp.bfloat16
            )

    def live_factor(tick):
        front = gx + gy - tick
        met = jnp.int32(0)
        for b in range(fronts.shape[0]):
            met = met | (fronts[b] == front).astype(jnp.int32)
        return met.astype(jnp.float32)

    def transfer(tick, h, index):
        _, low, high, dx, dy = parts[index]
        return pltpu.make_async_remote_copy(
            src_ref=sent.at[tick, h, pl.ds(low, high - low)],
            dst_ref=landed.at[tick, h, pl.ds(low, high - low)],
            send_sem=send_sem.at[tick, h, index],
            recv_sem=land_sem.at[tick, h, index],
            device_id=(gx + dx, gy + dy),
            device_id_type=MESH,
        )

    def send(tick, h, index):
        @pl.when(goes(*parts[index][3:]))
        def _():
            transfer(tick, h, index).start()

    def arrive(tick, h):
        for index in range(len(parts)):
            @pl.when(comes(*parts[index][3:]))
            def _(index=index):
                transfer(tick, h, index).wait_recv()

    def send_ready(tick, h, done):
        for index, (_, low, high, _, _) in enumerate(parts):
            if index not in done[1] and all(b in done[0] for b in range(low, high)):
                send(tick, h, index)
                done[1].add(index)

    enter_copy.wait()
    rounded = first_in[...].astype(jnp.bfloat16)
    live = live_factor(0)
    source_copies[0].wait()
    done = (set(), set())
    waited = False
    for start in tiles:
        green_copies[start].wait()
        product = jnp.dot(operator[start:start + TILE, :], rounded, preferred_element_type=jnp.float32)
        if start < edge:
            product = product + source_rows[0, start:start + TILE, :].astype(jnp.float32)
        out = (product * live).astype(jnp.bfloat16).T
        for q in range(TILE // LANES):
            block = start // LANES + q
            for h in range(HALVES):
                sent[0, h, block] = out[h * half:(h + 1) * half, q * LANES:(q + 1) * LANES]
            done[0].add(block)
        if not waited and all(b in done[0] for b in range(parts[0][1], parts[0][2])):
            count = sum(goes(dx, dy).astype(jnp.int32) for _, _, _, dx, dy in parts)

            @pl.when(count > 0)
            def _():
                pl.semaphore_wait(barrier, count)
            waited = True
        if waited:
            send_ready(0, 0, done)
    for h in range(1, HALVES):
        for index in range(len(parts)):
            send(0, h, index)

    for start in tiles:
        turned[:, start:start + TILE] = operator[start:start + TILE, :].T
    for tick in range(1, ticks):
        source_copies[tick].wait()
        if tick < ticks - 1:
            source_cols[tick] = source_rows[tick].T

    for tick in range(1, ticks - 1):
        live = live_factor(tick)
        for h in range(HALVES):
            arrive(tick - 1, h)
            incoming = jnp.concatenate([landed[tick - 1, h, b] for b in range(blocks)], axis=1)
            done = (set(), set())
            for start in tiles:
                product = jnp.dot(incoming, turned[:, start:start + TILE], preferred_element_type=jnp.float32)
                if start < edge:
                    product = product + source_cols[
                        tick, h * half:(h + 1) * half, start:start + TILE
                    ].astype(jnp.float32)
                out = (product * live).astype(jnp.bfloat16)
                for q in range(TILE // LANES):
                    block = start // LANES + q
                    sent[tick, h, block] = out[:, q * LANES:(q + 1) * LANES]
                    done[0].add(block)
                send_ready(tick, h, done)

    tick = ticks - 1
    live = live_factor(tick)
    for h in range(HALVES):
        arrive(tick - 1, h)
        incoming = jnp.concatenate([landed[tick - 1, h, b] for b in range(blocks)], axis=1)
        for index, start in enumerate(tiles):
            product = jnp.dot(incoming, turned[:, start:start + TILE], preferred_element_type=jnp.float32)
            held_half[h * half:(h + 1) * half, start:start + TILE] = product
            if h == HALVES - 1:
                whole = held_half[:, start:start + TILE].T
                if start < edge:
                    whole = whole + source_rows[tick, start:start + TILE, :].astype(jnp.float32)
                result[start:start + TILE, :] = whole * live
                pltpu.make_async_copy(
                    result.at[pl.ds(start, TILE)], last.at[0, 0, pl.ds(start, TILE)], last_sem.at[index]
                ).start()
    for index, start in enumerate(tiles):
        pltpu.make_async_copy(
            result.at[pl.ds(start, TILE)], last.at[0, 0, pl.ds(start, TILE)], last_sem.at[index]
        ).wait()
    for tick in range(ticks - 1):
        for h in range(HALVES):
            for index in range(len(parts)):
                @pl.when(goes(*parts[index][3:]))
                def _(tick=tick, h=h, index=index):
                    transfer(tick, h, index).wait_send()


def local(green, sources, entering, start_front):
    ticks, edge = sources.shape[0], sources.shape[3]
    order, width = entering.shape[2], entering.shape[3]
    half, blocks = width // HALVES, order // LANES
    n_tiles = order // TILE

    def body(*refs):
        sweep_kernel(ticks, order, edge // 2, width, *refs)

    hbm = pl.BlockSpec(memory_space=pltpu.HBM)
    return pl.pallas_call(
        body,
        name="sweep",
        out_shape=jax.ShapeDtypeStruct(entering.shape, jnp.float32),
        in_specs=[pl.BlockSpec(memory_space=pltpu.SMEM), hbm, hbm, hbm],
        out_specs=hbm,
        scratch_shapes=[
            pltpu.VMEM((order, order), jnp.bfloat16),
            pltpu.VMEM((order, order), jnp.bfloat16),
            pltpu.VMEM((ticks, edge, width), jnp.bfloat16),
            pltpu.VMEM((ticks, width, edge), jnp.bfloat16),
            pltpu.VMEM((order, width), jnp.float32),
            pltpu.VMEM((ticks - 1, HALVES, blocks, half, LANES), jnp.bfloat16),
            pltpu.VMEM((ticks - 1, HALVES, blocks, half, LANES), jnp.bfloat16),
            pltpu.VMEM((width, order), jnp.float32),
            pltpu.VMEM((order, width), jnp.float32),
            pltpu.SemaphoreType.DMA((n_tiles,)),
            pltpu.SemaphoreType.DMA((ticks,)),
            pltpu.SemaphoreType.DMA,
            pltpu.SemaphoreType.DMA((n_tiles,)),
            pltpu.SemaphoreType.DMA((ticks - 1, HALVES, 3)),
            pltpu.SemaphoreType.DMA((ticks - 1, HALVES, 3)),
        ],
        compiler_params=pltpu.CompilerParams(
            collective_id=0, has_side_effects=True, vmem_limit_bytes=56 * 1024 * 1024
        ),
        cost_estimate=pl.CostEstimate(
            flops=2 * ticks * order * order * width,
            bytes_accessed=2 * order * order + 2 * ticks * edge * width + 8 * order * width,
            transcendentals=0,
        ),
    )(start_front, green, sources, entering)


def solution(mesh):
    in_specs = (
        P("gx", "gy", None, None),
        P(None, "gx", "gy", None, None),
        P("gx", "gy", None, None),
        P(),
    )
    out_specs = P("gx", "gy", None, None)
    return jax.shard_map(local, mesh=mesh, in_specs=in_specs, out_specs=out_specs, check_vma=False)
```

time: 108 us -> 39.6 us (0.37)
  the two profiles are of different devices: /device:TPU:144 before, /device:TPU:504 now
where the time goes in v1:
time: 39.6 us; the launch traced here: 39.4 us
  Pallas kernels  37.5 us (95%)
  local copies, waits for them, and re-layouts  1.87 us (5%)
    pallas_call x1, Pallas kernels, local(): pl.pallas_call(body, name='sweep', out_shape=jax.ShapeDtypeStruct(enterin...  37.5 us
    unnamed x1, local copies, waits for them, and re-layouts  1.87 us

profile of v1, /device:TPU:504, one launch (start us, length us, event | category | flops | bytes accessed | tf_op | source)
XLA Modules:
  0.0 39.4 jit_solution(17604602701391432325)
XLA Ops:
  0.0 37.5 %sweep.1 = f32[1,1,1024,128]{3,2,1,0:T(8,128)} custom-call(s32[24]{0:T(128)} %refs_0_.1, bf16[1,1,1024,1024]{3,2,1,0:T(8,128)(2,1)} %refs_1_.1, bf16[6,1,1,768,128]{4,3,2,1,0:T(8,128)(2,1)} %refs_2_.1, f32[1,1,1024,128]{3,2,1,0:T(8,128)} %refs_3_.1), custom_call_target="tpu_custom_call" | custom-call | flops 1610612736 | bytes 4325376 | tf_op jit(solution)/shard_map/sweep/pallas_call | solution.py:206
  37.6 1.9 %copy.6 = f32[1,1,1024,128]{3,2,1,0:T(8,128)} copy(f32[1,1,1024,128]{3,2,1,0:T(8,128)} %sweep.1) | data formatting | bytes 1048576

commit v2 on v1

v2 whole, which is shorter than its diff:
```python
import jax
import jax.numpy as jnp
from jax import lax
from jax.experimental import pallas as pl
from jax.experimental.pallas import tpu as pltpu
from jax.sharding import PartitionSpec as P

MESH = pl.DeviceIdType.MESH
LANES = 128
CHUNKS = 4
TILE = 256


def sweep_kernel(
    ticks, order, trace, width,
    fronts_hbm, green, sources, entering, last,
    fronts, operator, turned, source_rows, source_cols, first_in, sent, landed, held_chunk, zeros,
    front_sem, green_sem, source_sem, entering_sem, send_sem, land_sem,
):
    gx, gy = lax.axis_index("gx"), lax.axis_index("gy")
    columns, rows = lax.axis_size("gx"), lax.axis_size("gy")
    edge = 2 * trace
    size = width // CHUNKS
    blocks = order // LANES
    parts = (
        (trace // LANES, edge // LANES, 0, 1),
        (edge // LANES, blocks, 1, 1),
        (0, trace // LANES, 1, 0),
    )
    tiles = [start for start in range(0, order, TILE)]
    tiles = [s for s in tiles if s + TILE > trace] + [s for s in tiles if s + TILE <= trace]

    def goes(dx, dy):
        ok = [gx < columns - 1] * dx + [gy < rows - 1] * dy
        return ok[0] if len(ok) == 1 else jnp.logical_and(*ok)

    def comes(dx, dy):
        ok = [gx > 0] * dx + [gy > 0] * dy
        return ok[0] if len(ok) == 1 else jnp.logical_and(*ok)

    barrier = pltpu.get_barrier_semaphore()
    for _, _, dx, dy in parts:
        @pl.when(comes(dx, dy))
        def _(dx=dx, dy=dy):
            pl.semaphore_signal(barrier, inc=1, device_id=(gx - dx, gy - dy), device_id_type=MESH)

    enter_copy = pltpu.make_async_copy(entering.at[0, 0], first_in, entering_sem)
    front_copy = pltpu.make_async_copy(fronts_hbm, fronts, front_sem)
    green_copies = {
        start: pltpu.make_async_copy(
            green.at[0, 0, pl.ds(start, TILE)], operator.at[pl.ds(start, TILE)], green_sem.at[index]
        )
        for index, start in enumerate(tiles)
    }
    source_copies = [
        pltpu.make_async_copy(sources.at[tick, 0, 0], source_rows.at[tick], source_sem.at[tick])
        for tick in range(ticks)
    ]
    enter_copy.start()
    green_copies[tiles[0]].start()
    front_copy.start()
    source_copies[0].start()
    for start in tiles[1:]:
        green_copies[start].start()
    for tick in range(1, ticks):
        source_copies[tick].start()

    def live_factor(tick):
        front = gx + gy - tick
        met = jnp.int32(0)
        for b in range(fronts.shape[0]):
            met = met | (fronts[b] == front).astype(jnp.int32)
        return met.astype(jnp.float32)

    zeros[...] = jnp.zeros(zeros.shape, jnp.bfloat16)
    for low, high, dx, dy in parts:
        @pl.when(jnp.logical_not(comes(dx, dy)))
        def _(low=low, high=high):
            for tick in range(ticks - 1):
                for h in range(CHUNKS):
                    pltpu.make_async_copy(
                        zeros.at[pl.ds(0, high - low)], landed.at[tick, h, pl.ds(low, high - low)],
                        land_sem.at[tick, h],
                    ).start()

    def transfer(tick, h, index):
        low, high, dx, dy = parts[index]
        return pltpu.make_async_remote_copy(
            src_ref=sent.at[tick, h, pl.ds(low, high - low)],
            dst_ref=landed.at[tick, h, pl.ds(low, high - low)],
            send_sem=send_sem.at[index],
            recv_sem=land_sem.at[tick, h],
            device_id=(gx + dx, gy + dy),
            device_id_type=MESH,
        )

    def send(tick, h, index):
        @pl.when(goes(*parts[index][2:]))
        def _():
            transfer(tick, h, index).start()

    def arrive(tick, h):
        pltpu.make_async_copy(landed.at[tick, h], landed.at[tick, h], land_sem.at[tick, h]).wait()

    def send_ready(tick, h, done):
        for index, (low, high, _, _) in enumerate(parts):
            if index not in done[1] and all(b in done[0] for b in range(low, high)):
                send(tick, h, index)
                done[1].add(index)

    enter_copy.wait()
    rounded = first_in[...].astype(jnp.bfloat16)
    front_copy.wait()
    live = live_factor(0)
    source_copies[0].wait()
    done = (set(), set())
    waited = False
    for start in tiles:
        green_copies[start].wait()
        product = jnp.dot(operator[start:start + TILE, :], rounded, preferred_element_type=jnp.float32)
        if start < edge:
            product = product + source_rows[0, start:start + TILE, :].astype(jnp.float32)
        out = (product * live).astype(jnp.bfloat16).T
        for q in range(TILE // LANES):
            block = start // LANES + q
            for h in range(CHUNKS):
                sent[0, h, block] = out[h * size:(h + 1) * size, q * LANES:(q + 1) * LANES]
            done[0].add(block)
        if not waited and all(b in done[0] for b in range(parts[0][0], parts[0][1])):
            count = sum(goes(dx, dy).astype(jnp.int32) for _, _, dx, dy in parts)

            @pl.when(count > 0)
            def _():
                pl.semaphore_wait(barrier, count)
            waited = True
        if waited:
            send_ready(0, 0, done)
    for h in range(1, CHUNKS):
        for index in range(len(parts)):
            send(0, h, index)

    for start in tiles:
        turned[:, start:start + TILE] = operator[start:start + TILE, :].T

    for tick in range(1, ticks):
        source_copies[tick].wait()
        if tick < ticks - 1:
            source_cols[tick] = source_rows[tick].T

    for tick in range(1, ticks - 1):
        live = live_factor(tick)
        for h in range(CHUNKS):
            arrive(tick - 1, h)
            incoming = jnp.concatenate([landed[tick - 1, h, b] for b in range(blocks)], axis=1)
            done = (set(), set())
            for start in tiles:
                product = jnp.dot(incoming, turned[:, start:start + TILE], preferred_element_type=jnp.float32)
                if start < edge:
                    product = product + source_cols[
                        tick, h * size:(h + 1) * size, start:start + TILE
                    ].astype(jnp.float32)
                out = (product * live).astype(jnp.bfloat16)
                for q in range(TILE // LANES):
                    block = start // LANES + q
                    sent[tick, h, block] = out[:, q * LANES:(q + 1) * LANES]
                    done[0].add(block)
                send_ready(tick, h, done)

    tick = ticks - 1
    live = live_factor(tick)
    for h in range(CHUNKS):
        if h == CHUNKS - 1:
            for index, (low, high, dx, dy) in enumerate(parts):
                @pl.when(goes(dx, dy))
                def _(low=low, high=high, index=index):
                    whole = sent.at[:, :, pl.ds(low, high - low)]
                    pltpu.make_async_copy(whole, whole, send_sem.at[index]).wait()
        arrive(tick - 1, h)
        incoming = jnp.concatenate([landed[tick - 1, h, b] for b in range(blocks)], axis=1)
        for start in tiles:
            product = jnp.dot(incoming, turned[:, start:start + TILE], preferred_element_type=jnp.float32)
            if h < CHUNKS - 1:
                held_chunk[h * size:(h + 1) * size, start:start + TILE] = product
            else:
                held = held_chunk[:, start:start + TILE]
                whole = jnp.concatenate([held, product], axis=0).T
                if start < edge:
                    whole = whole + source_rows[tick, start:start + TILE, :].astype(jnp.float32)
                last[0, 0, start:start + TILE, :] = whole * live


def local(green, sources, entering, start_front):
    ticks, edge = sources.shape[0], sources.shape[3]
    order, width = entering.shape[2], entering.shape[3]
    size, blocks = width // CHUNKS, order // LANES
    n_tiles = order // TILE

    def body(*refs):
        sweep_kernel(ticks, order, edge // 2, width, *refs)

    hbm = pl.BlockSpec(memory_space=pltpu.HBM)
    return pl.pallas_call(
        body,
        name="sweep",
        out_shape=jax.ShapeDtypeStruct(entering.shape, jnp.float32),
        in_specs=[hbm, hbm, hbm, hbm],
        out_specs=pl.BlockSpec(memory_space=pltpu.VMEM),
        scratch_shapes=[
            pltpu.SMEM(start_front.shape, jnp.int32),
            pltpu.VMEM((order, order), jnp.bfloat16),
            pltpu.VMEM((order, order), jnp.bfloat16),
            pltpu.VMEM((ticks, edge, width), jnp.bfloat16),
            pltpu.VMEM((ticks, width, edge), jnp.bfloat16),
            pltpu.VMEM((order, width), jnp.float32),
            pltpu.VMEM((ticks - 1, CHUNKS, blocks, size, LANES), jnp.bfloat16),
            pltpu.VMEM((ticks - 1, CHUNKS, blocks, size, LANES), jnp.bfloat16),
            pltpu.VMEM((width - size, order), jnp.float32),
            pltpu.VMEM((edge // 2 // LANES, size, LANES), jnp.bfloat16),
            pltpu.SemaphoreType.DMA,
            pltpu.SemaphoreType.DMA((n_tiles,)),
            pltpu.SemaphoreType.DMA((ticks,)),
            pltpu.SemaphoreType.DMA,
            pltpu.SemaphoreType.DMA((3,)),
            pltpu.SemaphoreType.DMA((ticks - 1, CHUNKS)),
        ],
        compiler_params=pltpu.CompilerParams(
            collective_id=0, has_side_effects=True, vmem_limit_bytes=54600 * 1024
        ),
        cost_estimate=pl.CostEstimate(
            flops=2 * ticks * order * order * width,
            bytes_accessed=2 * order * order + 2 * ticks * edge * width + 8 * order * width,
            transcendentals=0,
        ),
    )(start_front, green, sources, entering)


def solution(mesh):
    in_specs = (
        P("gx", "gy", None, None),
        P(None, "gx", "gy", None, None),
        P("gx", "gy", None, None),
        P(),
    )
    out_specs = P("gx", "gy", None, None)
    return jax.shard_map(local, mesh=mesh, in_specs=in_specs, out_specs=out_specs, check_vma=False)
```

time: 39.6 us -> 34 us (0.86)
  the two profiles are of different devices: /device:TPU:504 before, /device:TPU:19 now
where the time goes in v2:
time: 34 us; the launch traced here: 33.9 us
  Pallas kernels  32.4 us (95%)
  local copies, waits for them, and re-layouts  1.45 us (4%)
    pallas_call x1, Pallas kernels, local(): pl.pallas_call(body, name='sweep', out_shape=jax.ShapeDtypeStruct(enterin...  32.4 us
    unnamed x3, local copies, waits for them, and re-layouts  1.45 us

profile of v2, /device:TPU:19, one launch (start us, length us, event | category | flops | bytes accessed | tf_op | source)
XLA Modules:
  0.0 33.9 jit_solution(6074636981629985116)
XLA Ops:
  0.0 0.0 copy-start
  0.0 0.7 %copy-done = s32[24]{0:T(128)S(1)} copy-done((s32[24]{0:T(128)S(1)}, s32[24]{0:T(128)}, u32[]{:S(2)}) %copy-start) | copy-done | bytes 120
  0.7 32.4 %sweep.1 = f32[1,1,1024,128]{3,2,1,0:T(8,128)S(1)} custom-call(s32[24]{0:T(128)S(1)} %copy-done, bf16[1,1,1024,1024]{3,2,1,0:T(8,128)(2,1)} %refs_1_.1, bf16[6,1,1,768,128]{4,3,2,1,0:T(8,128)(2,1)} %refs_2_.1, f32[1,1,1024,128]{3,2,1,0:T(8,128)} %refs_3_.1), custom_call_target="tpu_custom_call" | custom-call | flops 1610612736 | bytes 4325376 | tf_op jit(solution)/shard_map/sweep/pallas_call | solution.py:202
  33.1 0.8 %copy.6 = f32[1,1,1024,128]{3,2,1,0:T(8,128)} copy(f32[1,1,1024,128]{3,2,1,0:T(8,128)S(1)} %sweep.1) | data formatting | bytes 1048576
Async XLA Ops:
  0.0 0.7 %copy-start = (s32[24]{0:T(128)S(1)}, s32[24]{0:T(128)}, u32[]{:S(2)}) copy-start(s32[24]{0:T(128)} %refs_0_.1) | copy-start | bytes 292

commit v3 on v2

--- a/solution.py
+++ b/solution.py
@@ -7,7 +7,7 @@
 
 MESH = pl.DeviceIdType.MESH
 LANES = 128
-CHUNKS = 4
+CHUNKS = (32, 32, 32, 32)
 TILE = 256
 
 
@@ -20,7 +20,8 @@
     gx, gy = lax.axis_index("gx"), lax.axis_index("gy")
     columns, rows = lax.axis_size("gx"), lax.axis_size("gy")
     edge = 2 * trace
-    size = width // CHUNKS
+    offsets = [sum(CHUNKS[:h]) for h in range(len(CHUNKS))]
+    final = len(CHUNKS) - 1
     blocks = order // LANES
     parts = (
         (trace // LANES, edge // LANES, 0, 1),
@@ -72,22 +73,25 @@
             met = met | (fronts[b] == front).astype(jnp.int32)
         return met.astype(jnp.float32)
 
+    def place(h, low, high):
+        return pl.ds(offsets[h] * blocks + low * CHUNKS[h], (high - low) * CHUNKS[h])
+
     zeros[...] = jnp.zeros(zeros.shape, jnp.bfloat16)
     for low, high, dx, dy in parts:
         @pl.when(jnp.logical_not(comes(dx, dy)))
         def _(low=low, high=high):
             for tick in range(ticks - 1):
-                for h in range(CHUNKS):
+                for h, size in enumerate(CHUNKS):
                     pltpu.make_async_copy(
-                        zeros.at[pl.ds(0, high - low)], landed.at[tick, h, pl.ds(low, high - low)],
+                        zeros.at[pl.ds(0, (high - low) * size)], landed.at[tick, place(h, low, high)],
                         land_sem.at[tick, h],
                     ).start()
 
     def transfer(tick, h, index):
         low, high, dx, dy = parts[index]
         return pltpu.make_async_remote_copy(
-            src_ref=sent.at[tick, h, pl.ds(low, high - low)],
-            dst_ref=landed.at[tick, h, pl.ds(low, high - low)],
+            src_ref=sent.at[tick, place(h, low, high)],
+            dst_ref=landed.at[tick, place(h, low, high)],
             send_sem=send_sem.at[index],
             recv_sem=land_sem.at[tick, h],
             device_id=(gx + dx, gy + dy),
@@ -100,7 +104,8 @@
             transfer(tick, h, index).start()
 
     def arrive(tick, h):
-        pltpu.make_async_copy(landed.at[tick, h], landed.at[tick, h], land_sem.at[tick, h]).wait()
+        whole = landed.at[tick, place(h, 0, blocks)]
+        pltpu.make_async_copy(whole, whole, land_sem.at[tick, h]).wait()
 
     def send_ready(tick, h, done):
         for index, (low, high, _, _) in enumerate(parts):
@@ -123,8 +128,10 @@
         out = (product * live).astype(jnp.bfloat16).T
         for q in range(TILE // LANES):
             block = start // LANES + q
-            for h in range(CHUNKS):
-                sent[0, h, block] = out[h * size:(h + 1) * size, q * LANES:(q + 1) * LANES]
+            for h, size in enumerate(CHUNKS):
+                sent[0, place(h, block, block + 1)] = out[
+                    offsets[h]:offsets[h] + size, q * LANES:(q + 1) * LANES
+                ]
             done[0].add(block)
         if not waited and all(b in done[0] for b in range(parts[0][0], parts[0][1])):
             count = sum(goes(dx, dy).astype(jnp.int32) for _, _, dx, dy in parts)
@@ -135,8 +142,8 @@
             waited = True
         if waited:
             send_ready(0, 0, done)
-    for h in range(1, CHUNKS):
-        for index in range(len(parts)):
+    for index in range(len(parts)):
+        for h in range(1, len(CHUNKS)):
             send(0, h, index)
 
     for start in tiles:
@@ -149,38 +156,38 @@
 
     for tick in range(1, ticks - 1):
         live = live_factor(tick)
-        for h in range(CHUNKS):
+        for h, size in enumerate(CHUNKS):
             arrive(tick - 1, h)
-            incoming = jnp.concatenate([landed[tick - 1, h, b] for b in range(blocks)], axis=1)
+            incoming = jnp.concatenate([landed[tick - 1, place(h, b, b + 1)] for b in range(blocks)], axis=1)
             done = (set(), set())
             for start in tiles:
                 product = jnp.dot(incoming, turned[:, start:start + TILE], preferred_element_type=jnp.float32)
                 if start < edge:
                     product = product + source_cols[
-                        tick, h * size:(h + 1) * size, start:start + TILE
+                        tick, offsets[h]:offsets[h] + size, start:start + TILE
                     ].astype(jnp.float32)
                 out = (product * live).astype(jnp.bfloat16)
                 for q in range(TILE // LANES):
                     block = start // LANES + q
-                    sent[tick, h, block] = out[:, q * LANES:(q + 1) * LANES]
+                    sent[tick, place(h, block, block + 1)] = out[:, q * LANES:(q + 1) * LANES]
                     done[0].add(block)
                 send_ready(tick, h, done)
 
     tick = ticks - 1
     live = live_factor(tick)
-    for h in range(CHUNKS):
-        if h == CHUNKS - 1:
+    for h, size in enumerate(CHUNKS):
+        if h == final:
             for index, (low, high, dx, dy) in enumerate(parts):
                 @pl.when(goes(dx, dy))
                 def _(low=low, high=high, index=index):
-                    whole = sent.at[:, :, pl.ds(low, high - low)]
+                    whole = sent.at[:, pl.ds(0, (high - low) * width)]
                     pltpu.make_async_copy(whole, whole, send_sem.at[index]).wait()
         arrive(tick - 1, h)
-        incoming = jnp.concatenate([landed[tick - 1, h, b] for b in range(blocks)], axis=1)
+        incoming = jnp.concatenate([landed[tick - 1, place(h, b, b + 1)] for b in range(blocks)], axis=1)
         for start in tiles:
             product = jnp.dot(incoming, turned[:, start:start + TILE], preferred_element_type=jnp.float32)
-            if h < CHUNKS - 1:
-                held_chunk[h * size:(h + 1) * size, start:start + TILE] = product
+            if h < final:
+                held_chunk[offsets[h]:offsets[h] + size, start:start + TILE] = product
             else:
                 held = held_chunk[:, start:start + TILE]
                 whole = jnp.concatenate([held, product], axis=0).T
@@ -192,7 +199,7 @@
 def local(green, sources, entering, start_front):
     ticks, edge = sources.shape[0], sources.shape[3]
     order, width = entering.shape[2], entering.shape[3]
-    size, blocks = width // CHUNKS, order // LANES
+    blocks = order // LANES
     n_tiles = order // TILE
 
     def body(*refs):
@@ -212,26 +219,26 @@
             pltpu.VMEM((ticks, edge, width), jnp.bfloat16),
             pltpu.VMEM((ticks, width, edge), jnp.bfloat16),
             pltpu.VMEM((order, width), jnp.float32),
-            pltpu.VMEM((ticks - 1, CHUNKS, blocks, size, LANES), jnp.bfloat16),
-            pltpu.VMEM((ticks - 1, CHUNKS, blocks, size, LANES), jnp.bfloat16),
-            pltpu.VMEM((width - size, order), jnp.float32),
-            pltpu.VMEM((edge // 2 // LANES, size, LANES), jnp.bfloat16),
+            pltpu.VMEM((ticks - 1, blocks * width, LANES), jnp.bfloat16),
+            pltpu.VMEM((ticks - 1, blocks * width, LANES), jnp.bfloat16),
+            pltpu.VMEM((width - CHUNKS[-1], order), jnp.float32),
+            pltpu.VMEM((edge // 2 // LANES * max(CHUNKS), LANES), jnp.bfloat16),
             pltpu.SemaphoreType.DMA,
             pltpu.SemaphoreType.DMA((n_tiles,)),
             pltpu.SemaphoreType.DMA((ticks,)),
             pltpu.SemaphoreType.DMA,
             pltpu.SemaphoreType.DMA((3,)),
-            pltpu.SemaphoreType.DMA((ticks - 1, CHUNKS)),
+            pltpu.SemaphoreType.DMA((ticks - 1, len(CHUNKS))),
         ],
         compiler_params=pltpu.CompilerParams(
-            collective_id=0, has_side_effects=True, vmem_limit_bytes=54600 * 1024
+            collective_id=0, has_side_effects=True, vmem_limit_bytes=32 * 1024 * 1024
         ),
         cost_estimate=pl.CostEstimate(
             flops=2 * ticks * order * order * width,
             bytes_accessed=2 * order * order + 2 * ticks * edge * width + 8 * order * width,
             transcendentals=0,
         ),
-    )(start_front, green, sources, entering)
+    )(*(pltpu.with_memory_space_constraint(a, pltpu.HBM) for a in (start_front, green, sources, entering)))
 
 
 def solution(mesh):

time: 34 us -> 32.9 us (0.968)
  the two profiles are of different devices: /device:TPU:19 before, /device:TPU:504 now
where the time goes in v3:
time: 32.9 us; the launch traced here: 32.3 us
  Pallas kernels  31.5 us (96%)
  local copies, waits for them, and re-layouts  0.8 us (2%)
    pallas_call x1, Pallas kernels, local(): pl.pallas_call(body, name='sweep', out_shape=jax.ShapeDtypeStruct(enterin...  31.5 us
    unnamed x1, local copies, waits for them, and re-layouts  0.8 us

profile of v3, /device:TPU:504, one launch (start us, length us, event | category | flops | bytes accessed | tf_op | source)
XLA Modules:
  0.0 32.3 jit_solution(6577826093536159000)
XLA Ops:
  0.0 31.5 %sweep.1 = f32[1,1,1024,128]{3,2,1,0:T(8,128)S(1)} custom-call(s32[24]{0:T(128)} %refs_0_.1, bf16[1,1,1024,1024]{3,2,1,0:T(8,128)(2,1)} %refs_1_.1, bf16[6,1,1,768,128]{4,3,2,1,0:T(8,128)(2,1)} %refs_2_.1, f32[1,1,1024,128]{3,2,1,0:T(8,128)} %refs_3_.1), custom_call_target="tpu_custom_call" | custom-call | flops 1610612736 | bytes 4325376 | tf_op jit(solution)/shard_map/sweep/pallas_call | solution.py:209
  31.5 0.8 %copy.6 = f32[1,1,1024,128]{3,2,1,0:T(8,128)} copy(f32[1,1,1024,128]{3,2,1,0:T(8,128)S(1)} %sweep.1) | data formatting | bytes 1048576

commit v4 on v3

--- a/solution.py
+++ b/solution.py
@@ -38,6 +38,9 @@
     def comes(dx, dy):
         ok = [gx > 0] * dx + [gy > 0] * dy
         return ok[0] if len(ok) == 1 else jnp.logical_and(*ok)
+
+    to_next = [goes(dx, dy) for _, _, dx, dy in parts]
+    next_device = [(gx + dx, gy + dy) for _, _, dx, dy in parts]
 
     barrier = pltpu.get_barrier_semaphore()
     for _, _, dx, dy in parts:
@@ -88,20 +91,30 @@
                     ).start()
 
     def transfer(tick, h, index):
-        low, high, dx, dy = parts[index]
+        low, high, _, _ = parts[index]
         return pltpu.make_async_remote_copy(
             src_ref=sent.at[tick, place(h, low, high)],
             dst_ref=landed.at[tick, place(h, low, high)],
             send_sem=send_sem.at[index],
             recv_sem=land_sem.at[tick, h],
-            device_id=(gx + dx, gy + dy),
+            device_id=next_device[index],
             device_id_type=MESH,
         )
 
     def send(tick, h, index):
-        @pl.when(goes(*parts[index][2:]))
-        def _():
-            transfer(tick, h, index).start()
+        ok = to_next[index]
+        if index == 0:
+            @pl.when(jnp.logical_and(ok, gx % 2 == 0))
+            def _():
+                transfer(tick, h, index).start()
+        else:
+            @pl.when(ok)
+            def _():
+                transfer(tick, h, index).start()
+        if index == 1:
+            @pl.when(jnp.logical_and(goes(0, 1), gx % 2 == 1))
+            def _():
+                transfer(tick, h, 0).start()
 
     def arrive(tick, h):
         whole = landed.at[tick, place(h, 0, blocks)]

time: 32.9 us -> 32.9 us (level)
  no operation moved by 1% of the time
where the time goes in v4:
time: 32.9 us; the launch traced here: 32.3 us
  Pallas kernels  31.5 us (96%)
  local copies, waits for them, and re-layouts  0.8 us (2%)
    pallas_call x1, Pallas kernels, local(): pl.pallas_call(body, name='sweep', out_shape=jax.ShapeDtypeStruct(enterin...  31.5 us
    unnamed x1, local copies, waits for them, and re-layouts  0.8 us

profile of v4, /device:TPU:504, one launch (start us, length us, event | category | flops | bytes accessed | tf_op | source)
XLA Modules:
  0.0 32.3 jit_solution(7241408496303482492)
XLA Ops:
  0.0 31.5 %sweep.1 = f32[1,1,1024,128]{3,2,1,0:T(8,128)S(1)} custom-call(s32[24]{0:T(128)} %refs_0_.1, bf16[1,1,1024,1024]{3,2,1,0:T(8,128)(2,1)} %refs_1_.1, bf16[6,1,1,768,128]{4,3,2,1,0:T(8,128)(2,1)} %refs_2_.1, f32[1,1,1024,128]{3,2,1,0:T(8,128)} %refs_3_.1), custom_call_target="tpu_custom_call" | custom-call | flops 1610612736 | bytes 4325376 | tf_op jit(solution)/shard_map/sweep/pallas_call | solution.py:222
  31.5 0.8 %copy.6 = f32[1,1,1024,128]{3,2,1,0:T(8,128)} copy(f32[1,1,1024,128]{3,2,1,0:T(8,128)S(1)} %sweep.1) | data formatting | bytes 1048576

commit v5 on v4

--- a/solution.py
+++ b/solution.py
@@ -156,7 +156,9 @@
         if waited:
             send_ready(0, 0, done)
     for index in range(len(parts)):
-        for h in range(1, len(CHUNKS)):
+        send(0, 1, index)
+    for index in range(len(parts)):
+        for h in range(2, len(CHUNKS)):
             send(0, h, index)
 
     for start in tiles:

time: 32.9 us -> 33.2 us (level)
  the two profiles are of different devices: /device:TPU:504 before, /device:TPU:19 now
where the time goes in v5:
time: 33.2 us; the launch traced here: 33.1 us
  Pallas kernels  32.3 us (97%)
  local copies, waits for them, and re-layouts  0.8 us (2%)
    pallas_call x1, Pallas kernels, local(): pl.pallas_call(body, name='sweep', out_shape=jax.ShapeDtypeStruct(enterin...  32.3 us
    unnamed x1, local copies, waits for them, and re-layouts  0.8 us

profile of v5, /device:TPU:19, one launch (start us, length us, event | category | flops | bytes accessed | tf_op | source)
XLA Modules:
  0.0 33.1 jit_solution(501795441565609426)
XLA Ops:
  0.0 32.3 %sweep.1 = f32[1,1,1024,128]{3,2,1,0:T(8,128)S(1)} custom-call(s32[24]{0:T(128)} %refs_0_.1, bf16[1,1,1024,1024]{3,2,1,0:T(8,128)(2,1)} %refs_1_.1, bf16[6,1,1,768,128]{4,3,2,1,0:T(8,128)(2,1)} %refs_2_.1, f32[1,1,1024,128]{3,2,1,0:T(8,128)} %refs_3_.1), custom_call_target="tpu_custom_call" | custom-call | flops 1610612736 | bytes 4325376 | tf_op jit(solution)/shard_map/sweep/pallas_call | solution.py:224
  32.3 0.8 %copy.6 = f32[1,1,1024,128]{3,2,1,0:T(8,128)} copy(f32[1,1,1024,128]{3,2,1,0:T(8,128)S(1)} %sweep.1) | data formatting | bytes 1048576
